TPU v7x, 32 devices: a whole 2x2x4 slice. The times are simulated.
32 devices in a mesh: gx: 4 (over y, x), gy: 4 (over z), gz: 2 (over core).
Axes of the slice: x: 2, y: 2, z: 4, core: 2. Of those that a mesh axis runs over, the one named last changes fastest.
Arguments:
- positions: float32 [3, 32768], P(None, ('gx', 'gy', 'gz')), as said below
- polarizability: float32 [4, 2, 32768], P(None, None, ('gx', 'gy', 'gz')), may hold values from -0.5 to 1
- applied_field: float32 [4, 2, 3, 32768], P(None, None, None, ('gx', 'gy', 'gz')), may hold values from -6 to 6
- pair_codes: int32 [768], P(('gx', 'gy', 'gz')), may hold values from 0 to 1151
- pair_counts: int32 [32], P(('gx', 'gy', 'gz')), may hold values from 3 to 24, as said below
Outputs:
- dipoles: float32 [4, 2, 3, 32768], P(None, None, None, ('gx', 'gy', 'gz'))
Inputs may be any that keep to these rules, and one draw needn't show every extreme that they name: `pair_codes`: each code is ((dx + 1) * 3 + (dy + 1)) * 2 * 8^2 + zt * 8^2 + target_block * 8 + source_block with dx, dy in -1..1, zt in 0..1 and blocks in 0..7; only the first pair_counts entries of a device's list are live. `pair_counts`: some device has 24 live entries in every draw. `positions`: x and y lie in [0, 4) within the owner's slab cell; z lies in [2 z_half, 2 z_half + 2) for the owner's depth half.
All inputs are finite; a program needn't handle non-finite values.
Results may differ from a plain program's by a relative error of at most 0.0003.
Values sent between devices are 32-bit elements; how exact they have to be, the bound alone decides.
A program may use at most 64 MiB of HBM per device.

v0:
```python
import math

import jax
import jax.numpy as jnp
from jax import lax
from jax.sharding import PartitionSpec as P

BLOCK = 128
ITERS = 4


cell_width = 4.0
soften = 1.0
screen = 0.5
coupling = 0.8


def from_behind(value, axis, steps):
    count = lax.axis_size(axis)
    pairs = [(source, (source + steps) % count) for source in range(count)]
    return lax.ppermute(value, axis, pairs)


def padded(block, sides, width):
    for axis, dim in sides:
        count = lax.axis_size(axis)
        forward = [(i, i + 1) for i in range(count - 1)]
        forward.append((count - 1, 0))
        backward = [(target, source) for source, target in forward]
        low = lax.ppermute(
            lax.slice_in_dim(block, block.shape[dim] - width, None, axis=dim), axis, forward
        )
        high = lax.ppermute(lax.slice_in_dim(block, 0, width, axis=dim), axis, backward)
        block = jnp.concatenate([low, block, high], axis=dim)
    return block


def tensor_field(tgt_pos, src_pos, shift_x, shift_y, sources):
    disp_x = tgt_pos[0][:, None] - src_pos[0][None, :] + shift_x
    disp_y = tgt_pos[1][:, None] - src_pos[1][None, :] + shift_y
    disp_z = tgt_pos[2][:, None] - src_pos[2][None, :]
    dist_sq = disp_x * disp_x + disp_y * disp_y + disp_z * disp_z + soften * soften
    inv_dist = lax.rsqrt(dist_sq)
    distance = dist_sq * inv_dist
    screened = jax.scipy.special.erfc(screen * distance)
    gaussian = 2.0 * screen / math.sqrt(math.pi) * jnp.exp(-screen * screen * dist_sq)
    inv_sq = inv_dist * inv_dist
    b_term = screened * inv_sq * inv_dist + gaussian * inv_sq
    c_term = (
        3.0 * screened * inv_sq * inv_dist + gaussian * (2.0 * screen * screen + 3.0 * inv_sq)
    ) * inv_sq
    disp_vec = jnp.stack([disp_x, disp_y, disp_z])
    tensor = (
        c_term[None, :, None, :]
        * disp_vec[:, :, None, :]
        * jnp.transpose(disp_vec, (1, 0, 2))[None, :, :, :]
    )
    tensor = tensor - jnp.eye(3, dtype=tensor.dtype)[:, None, :, None] * b_term[None, :, None, :]
    block_len = tgt_pos.shape[1]
    matrix = tensor.reshape(3 * block_len, 3 * block_len)
    flat_src = sources.reshape(-1, 3 * block_len)
    result = lax.dot_general(
        flat_src,
        matrix,
        (((1,), (1,)), ((), ())),
        precision=lax.Precision.HIGHEST,
        preferred_element_type=jnp.float32,
    )
    return result.reshape(sources.shape)


def carry(lower_part, upper_part):
    from_above = from_behind(lower_part, "gy", -1)
    from_below = from_behind(upper_part, "gy", 1)
    return from_above + from_below


def depth_sum(partial_value):
    return lax.psum_scatter(partial_value, "gz", scatter_dimension=3, tiled=True)


def shards(positions, polarizability, applied_field, pair_codes, pair_counts):
    freqs = polarizability.shape[0]
    local_rows = positions.shape[1]
    nblocks = local_rows // BLOCK
    square = nblocks * nblocks
    z_index = lax.axis_index("gz")
    pos_cube = positions.reshape(3, 1, 1, 1, local_rows)
    beside_all = padded(pos_cube, (("gx", 1), ("gy", 2), ("gz", 3)), 1)
    beside_all = beside_all.reshape(3, 27 * local_rows)
    a_re = polarizability[:, 0][:, None]
    a_im = polarizability[:, 1][:, None]

    def respond(field_re, field_im):
        return jnp.stack(
            [a_re * field_re - a_im * field_im, a_re * field_im + a_im * field_re], axis=1
        )

    def add_pair(partial_value, pair_code, sources, depth_src):
        src_block = pair_code % nblocks
        tgt_block = pair_code // nblocks % nblocks
        depth_tgt = pair_code // square % 2
        step_y = pair_code // (2 * square) % 3
        step_x = pair_code // (6 * square)
        src_start = (
            (step_x * 3 + 1) * 3 + depth_src - z_index + 1
        ) * local_rows + src_block * BLOCK
        tgt_start = ((3 + step_y) * 3 + depth_tgt - z_index + 1) * local_rows + tgt_block * BLOCK
        src_pos = lax.dynamic_slice_in_dim(beside_all, src_start, BLOCK, 1)
        tgt_pos = lax.dynamic_slice_in_dim(beside_all, tgt_start, BLOCK, 1)
        src_dip = lax.dynamic_slice_in_dim(
            sources, step_x * local_rows + src_block * BLOCK, BLOCK, 3
        )
        shift_x = (step_x - 1).astype(jnp.float32) * -cell_width
        shift_y = (step_y - 1).astype(jnp.float32) * cell_width
        contrib = tensor_field(tgt_pos, src_pos, shift_x, shift_y, src_dip)
        out_start = ((depth_tgt * 3 + step_y) * nblocks + tgt_block) * BLOCK
        previous = lax.dynamic_slice_in_dim(partial_value, out_start, BLOCK, 3)
        return lax.dynamic_update_slice_in_dim(partial_value, previous + contrib, out_start, 3)

    dipoles = respond(applied_field[:, 0], applied_field[:, 1])
    for sweep in range(ITERS):
        sources = padded(dipoles, (("gx", 3),), local_rows)
        partial_value = jnp.zeros((freqs, 2, 3, 6 * local_rows), jnp.float32)

        def own_entry(entry, partial_value):
            return add_pair(partial_value, pair_codes[entry], sources, z_index)

        partial_value = lax.fori_loop(0, pair_counts[0], own_entry, partial_value)
        partial_value = partial_value.reshape(freqs, 2, 3, 2, 3, local_rows)
        summed = depth_sum(partial_value)[:, :, :, 0]
        field = summed[:, :, :, 1] + carry(summed[:, :, :, 0], summed[:, :, :, 2])
        dipoles = respond(
            applied_field[:, 0] + coupling * field[:, 0],
            applied_field[:, 1] + coupling * field[:, 1],
        )
    return dipoles


def solution(mesh):
    in_specs = (
        P(None, ("gx", "gy", "gz")),
        P(None, None, ("gx", "gy", "gz")),
        P(None, None, None, ("gx", "gy", "gz")),
        P(("gx", "gy", "gz")),
        P(("gx", "gy", "gz")),
    )
    out_specs = P(None, None, None, ("gx", "gy", "gz"))
    return jax.shard_map(shards, mesh=mesh, in_specs=in_specs, out_specs=out_specs, check_vma=False)
```

profile of v0, /device:TPU:0, one launch (start us, length us, event | category | flops | bytes accessed | tf_op | source)
XLA Modules:
  0.0 817.9 jit_solution(739892063358397272)
XLA Ops:
  6.5 2.9 collective-permute-start.2
  25.3 47.5 %while.52 = (s32[]{:T(128)}, f32[4,2,3,6144]{3,0,2,1:T(4,128)S(1)}, s32[]{:T(128)}, s32[24]{0:T(128)S(1)}, f32[4,2,3,3072]{3,0,2,1:T(4,128)S(1)}, /*index=5*/s32...) while((s32[]{:T(128)}, f32[4,2,3,6144]{3,0,2,1:T(4,128)S(1)}, ...), condition=%wide.region_1.2_spmd, body=%wide.region_0.1_spmd.sunk | while | flops 16272520 | bytes 1500673 | solution.py:129
  75.0 130.3 %all-reduce.9.cloned.1.call-done = f32[4,2,3,2,3,1024]{5,0,4,3,2,1:T(4,128)} async-done(((f32[4,2,3,2,3,1024]{5,0,4,3,2,1:T(4,128)}), f32[4,2,3,2,3,1024]{5,0,4,3,2,1:T(4,128)}) %all-reduce.9.cloned.1.call-update) | async-done | bytes 589840
  206.9 3.7 collective-permute-start.8
  210.6 3.2 collective-permute-done.8
  213.7 3.3 collective-permute-done.9
  220.2 3.0 collective-permute-done.10
  224.3 47.5 %while.53 = (s32[]{:T(128)}, f32[4,2,3,6144]{3,0,2,1:T(4,128)S(1)}, s32[]{:T(128)}, s32[24]{0:T(128)S(1)}, f32[4,2,3,3072]{3,0,2,1:T(4,128)S(1)}, /*index=5*/s32...) while((s32[]{:T(128)}, f32[4,2,3,6144]{3,0,2,1:T(4,128)S(1)}, ...), condition=%wide.region_4.5_spmd, body=%wide.region_3.4_spmd.sunk | while | flops 16272520 | bytes 1500673 | solution.py:129
  272.7 130.4 %all-reduce.11.cloned.1.call-done = f32[4,2,3,2,3,1024]{5,0,2,1,4,3:T(4,128)} async-done(((f32[4,2,3,2,3,1024]{5,0,2,1,4,3:T(4,128)}), f32[4,2,3,2,3,1024]{5,0,2,1,4,3:T(4,128)}) %all-reduce.11.cloned.1.call-update) | async-done | bytes 589840
  404.7 3.7 collective-permute-start.12
  408.4 3.2 collective-permute-done.12
  411.5 3.3 collective-permute-done.13
  418.0 3.0 collective-permute-done.14
  422.1 47.5 %while.54 = (s32[]{:T(128)}, f32[4,2,3,6144]{3,0,2,1:T(4,128)S(1)}, s32[]{:T(128)}, s32[24]{0:T(128)S(1)}, f32[4,2,3,3072]{3,0,2,1:T(4,128)S(1)}, /*index=5*/s32...) while((s32[]{:T(128)}, f32[4,2,3,6144]{3,0,2,1:T(4,128)S(1)}, ...), condition=%wide.region_7.8_spmd, body=%wide.region_6.7_spmd.sunk | while | flops 16272520 | bytes 1500673 | solution.py:129
  470.5 130.4 %all-reduce.13.cloned.1.call-done = f32[4,2,3,2,3,1024]{5,0,2,1,4,3:T(4,128)} async-done(((f32[4,2,3,2,3,1024]{5,0,2,1,4,3:T(4,128)}), f32[4,2,3,2,3,1024]{5,0,2,1,4,3:T(4,128)}) %all-reduce.13.cloned.1.call-update) | async-done | bytes 589840
  602.5 3.7 collective-permute-start.16
  606.2 3.2 collective-permute-done.16
  609.4 3.3 collective-permute-done.17
  615.8 3.0 collective-permute-done.18
  619.9 47.5 %while.55 = (s32[]{:T(128)}, f32[4,2,3,6144]{3,0,2,1:T(4,128)S(1)}, s32[]{:T(128)}, s32[24]{0:T(128)S(1)}, f32[4,2,3,3072]{3,0,2,1:T(4,128)S(1)}, /*index=5*/s32...) while((s32[]{:T(128)}, f32[4,2,3,6144]{3,0,2,1:T(4,128)S(1)}, ...), condition=%wide.region_10.11_spmd, body=%wide.region_9.10_spmd.sunk | while | flops 16272520 | bytes 1500673 | solution.py:129
  668.3 130.4 %all-reduce.15.cloned.1.call-done = f32[4,2,3,2,3,1024]{5,0,2,1,4,3:T(4,128)} async-done(((f32[4,2,3,2,3,1024]{5,0,2,1,4,3:T(4,128)}), f32[4,2,3,2,3,1024]{5,0,2,1,4,3:T(4,128)}) %all-reduce.15.cloned.1.call-update) | async-done | bytes 589840
  800.3 3.7 collective-permute-start.20
  804.0 3.2 collective-permute-done.20
  807.2 3.3 collective-permute-done.21
  (365 shorter events, 94.9 us)
Async XLA Ops:
  6.5 198.7 %all-reduce.9.cloned.1.call-start = ((), (), s32[]{:S(2)}) async-start(), calls=%async_computation | async-start | bytes 1179648
  6.5 5.9 collective-permute-start.2
  13.4 6.9 collective-permute-start.4
  15.2 5.1 collective-permute-start.5
  17.4 5.7 collective-permute-start
  19.8 4.6 collective-permute-start.1
  20.4 4.1 collective-permute-start.6
  73.6 329.5 %all-reduce.11.cloned.1.call-start = ((), (), s32[]{:S(2)}) async-start(), calls=%async_computation.1 | async-start | bytes 1179648
  206.9 6.8 collective-permute-start.8
  210.6 6.5 collective-permute-start.9
  217.2 6.0 collective-permute-start.10
  218.7 5.4 collective-permute-start.11
  272.6 328.2 %all-reduce.13.cloned.1.call-start = ((), (), s32[]{:S(2)}) async-start(), calls=%async_computation.2 | async-start | bytes 1179648
  404.7 6.8 collective-permute-start.12
  408.4 6.5 collective-permute-start.13
  415.0 6.0 collective-permute-start.14
  416.5 5.4 collective-permute-start.15
  470.5 328.2 %all-reduce.15.cloned.1.call-start = ((), (), s32[]{:S(2)}) async-start(), calls=%async_computation.3 | async-start | bytes 1179648
  602.5 6.8 collective-permute-start.16
  606.2 6.5 collective-permute-start.17
  612.8 6.0 collective-permute-start.18
  614.3 5.4 collective-permute-start.19
  800.3 6.8 collective-permute-start.20
  804.0 6.5 collective-permute-start.21
  (6 other events, 11.2 us)
Sparse Core Ops, SparseCore 0:
  73.7 131.4 all-reduce.8
  272.8 130.2 all-reduce.10
  470.6 130.2 all-reduce.12
  668.4 130.2 all-reduce.14
where the time goes:
time: 820 us; the launch traced here: 818 us
  waiting for transfers between devices  564 us (69%)
  loops' own time  135 us (16%)
  starting transfers between devices  35 us (4%)
  local copies, waits for them, and re-layouts  32.4 us (4%)
  matrix products  20.7 us (3%)
  other arithmetic  17.2 us (2%)
  between operations  13.5 us (2%)
    unnamed x8, waiting for transfers between devices  522 us
    another operation x4, loops' own time, shards(): partial_value = lax.fori_loop(0, pair_counts[0], own_entry, partial_value)  135 us
    ppermute x8, waiting for transfers between devices, from_behind(): return lax.ppermute(value, axis, pairs)  26 us
    dot_general x28, matrix products, tensor_field(): lax.dot_general(flat_src, matrix, (((1,), (1,)), ((), ())), precision=lax...  20.7 us
    dynamic_slice x28, local copies, waits for them, and re-layouts, own_entry(): return add_pair(partial_value, pair_codes[entry], sources, z_index)  17.2 us
  transfers between devices with their start and end apart: 26, of which 21 were waited for; matrix products, arithmetic and copies ran while one was open for 0% of the time, Pallas kernels for 0%

commit v1 on v0

v1 whole, which is shorter than its diff:
```python
import functools
import math

import jax
import jax.numpy as jnp
from jax import lax
from jax.experimental import pallas as pl
from jax.experimental.pallas import tpu as pltpu
from jax.sharding import PartitionSpec as P

BLOCK = 128
ITERS = 4
UNROLL = 4

cell_width = 4.0
soften = 1.0
screen = 0.5
coupling = 0.8

CENTER = 0.54
SERIES = (
    0.806488610702616,
    0.7241185361715909,
    0.27511941992319955,
    -0.26086845400919295,
    0.2296813716405795,
    -0.17763507721765817,
    0.1043247007059023,
    -0.02452746718798479,
    -0.07547989643924369,
    0.2975431845822381,
    -0.5276853186117066,
    0.345520543574722,
)
MESH = pl.DeviceIdType.MESH


def split(value):
    high = value.astype(jnp.bfloat16)
    low = (value - high.astype(jnp.float32)).astype(jnp.bfloat16)
    return high, low


def kernel(
    sizes,
    codes_ref,
    count_ref,
    pos_ref,
    a1_ref,
    a2_ref,
    field_ref,
    out_ref,
    src_pos,
    tgt_pos,
    tensors,
    choose,
    chosen,
    sources,
    halves,
    contribs,
    partial,
    depth_in,
    carry_in,
    pos_send,
    pos_recv,
    x_send,
    x_recv,
    z_send,
    z_recv,
    y_send,
    y_recv,
):
    n_x, n_y, nblocks, pairs = sizes
    square = nblocks * nblocks
    rows = field_ref.shape[1]
    x = lax.axis_index("gx")
    y = lax.axis_index("gy")
    z = lax.axis_index("gz")
    x_up, x_down = lax.rem(x + 1, n_x), lax.rem(x + n_x - 1, n_x)
    y_up, y_down = lax.rem(y + 1, n_y), lax.rem(y + n_y - 1, n_y)
    other = 1 - z

    barrier = pltpu.get_barrier_semaphore()
    partners = (
        (x_up, y, z),
        (x_down, y, z),
        (x, y_up, z),
        (x, y_down, z),
        (x, y_up, other),
        (x, y_down, other),
        (x, y, other),
    )
    for partner in partners:
        pl.semaphore_signal(barrier, inc=1, device_id=partner, device_id_type=MESH)

    def respond(field, block):
        turned = jnp.concatenate([field[rows // 2 :], field[: rows // 2]], axis=0)
        return a1_ref[block] * field + a2_ref[block] * turned

    for block in range(nblocks):
        for k in range(3):
            lanes = pl.ds(k * BLOCK, BLOCK)
            sources[0, 1, block, :, lanes] = respond(field_ref[block, :, lanes], block)
    src_pos[1] = pos_ref[...]
    tgt_pos[1] = pos_ref[...]

    def send(src, dst, send_sem, recv_sem, device):
        return pltpu.make_async_remote_copy(
            src_ref=src,
            dst_ref=dst,
            send_sem=send_sem,
            recv_sem=recv_sem,
            device_id=device,
            device_id_type=MESH,
        )

    pl.semaphore_wait(barrier, len(partners))

    def x_copies(sweep):
        return (
            send(sources.at[sweep, 1], sources.at[sweep, 0], x_send.at[sweep, 0], x_recv.at[sweep, 0], (x_up, y, z)),
            send(sources.at[sweep, 1], sources.at[sweep, 2], x_send.at[sweep, 1], x_recv.at[sweep, 1], (x_down, y, z)),
        )

    pos_copies = (
        send(pos_ref, src_pos.at[0], pos_send.at[0], pos_recv.at[0], (x_up, y, z)),
        send(pos_ref, src_pos.at[2], pos_send.at[1], pos_recv.at[1], (x_down, y, z)),
        send(pos_ref, tgt_pos.at[0], pos_send.at[2], pos_recv.at[2], (x, y_up, z)),
        send(pos_ref, tgt_pos.at[2], pos_send.at[3], pos_recv.at[3], (x, y_down, z)),
        send(pos_ref, tgt_pos.at[3], pos_send.at[4], pos_recv.at[4], (x, y_up, other)),
        send(pos_ref, tgt_pos.at[5], pos_send.at[5], pos_recv.at[5], (x, y_down, other)),
        send(pos_ref, tgt_pos.at[4], pos_send.at[6], pos_recv.at[6], (x, y, other)),
    )
    for copy in pos_copies:
        copy.start()
    for copy in x_copies(0):
        copy.start()
    for copy in pos_copies:
        copy.wait()

    def decode(entry):
        code = codes_ref[entry]
        src_block = code % nblocks
        tgt_block = code // nblocks % nblocks
        depth_tgt = code // square % 2
        step_y = code // (2 * square) % 3
        step_x = code // (6 * square)
        turned_depth = (depth_tgt + z) % 2
        return src_block, tgt_block, turned_depth, step_y, step_x

    def build(entry, carried):
        src_block, tgt_block, depth, step_y, step_x = decode(entry)
        src = src_pos[step_x, src_block].T
        tgt = tgt_pos[depth * 3 + step_y, tgt_block]
        shift_x = (step_x - 1).astype(jnp.float32) * -cell_width
        shift_y = (step_y - 1).astype(jnp.float32) * cell_width
        disp = [
            tgt[0:1] - src[:, 0:1] + shift_x,
            tgt[1:2] - src[:, 1:2] + shift_y,
            tgt[2:3] - src[:, 2:3],
        ]
        dist_sq = disp[0] * disp[0] + disp[1] * disp[1] + disp[2] * disp[2] + soften * soften
        inv = lax.rsqrt(dist_sq)
        inv_sq = inv * inv
        offset = inv - CENTER
        series = jnp.full_like(offset, SERIES[-1])
        for term in SERIES[-2::-1]:
            series = series * offset + term
        scale = jnp.exp(-screen * screen * dist_sq) * inv_sq
        b_term = scale * series
        c_term = scale * (3.0 * inv_sq * series + 2.0 * screen * screen / math.sqrt(math.pi))
        for a in range(3):
            scaled = c_term * disp[a]
            for b in range(a, 3):
                value = scaled * disp[b]
                if a == b:
                    value = value - b_term
                high, low = split(value)
                for r, c in {(a, b), (b, a)}:
                    lanes = pl.ds(c * BLOCK, BLOCK)
                    tensors[entry, pl.ds(r * BLOCK, BLOCK), lanes] = high
                    tensors[entry, pl.ds((3 + r) * BLOCK, BLOCK), lanes] = low
        slot = (depth * 3 + step_y) * nblocks + tgt_block
        slot = jnp.where(entry < count_ref[0], slot, -1)
        shape = (rows, 6 * nblocks * rows)
        column = lax.broadcasted_iota(jnp.int32, shape, 1)
        row = lax.broadcasted_iota(jnp.int32, shape, 0)
        choose[pl.ds(entry * rows, rows), :] = jnp.where(column == slot * rows + row, 1.0, 0.0)
        return carried

    lax.fori_loop(0, pairs, build, 0)
    chosen[...] = choose[...].T.astype(jnp.bfloat16)

    def sweep_step(sweep, carried):
        copies = x_copies(sweep)
        for copy in copies:
            copy.wait()
        for step in range(3):
            for block in range(nblocks):
                high, low = split(sources[sweep, step, block])
                halves[step, block] = jnp.concatenate([high, low], axis=0)

        def pair_step(group, carried):
            for member in range(UNROLL):
                entry = group * UNROLL + member
                src_block, _, _, _, step_x = decode(entry)
                both = halves[step_x, src_block]
                both = jnp.concatenate([both, both], axis=1)
                result = jnp.dot(both, tensors[entry], preferred_element_type=jnp.float32)
                contribs[pl.ds(entry * rows, rows), :] = result[:rows] + result[rows:]
            return carried

        lax.fori_loop(0, pairs // UNROLL, pair_step, 0)
        high, low = split(contribs[...])
        merged = jnp.dot(chosen[...], high, preferred_element_type=jnp.float32) + jnp.dot(
            chosen[...], low, preferred_element_type=jnp.float32
        )
        partial[sweep] = merged.reshape(6, nblocks, rows, 3 * BLOCK)

        z_copies = [
            send(
                partial.at[sweep, 3 + step],
                depth_in.at[sweep, step],
                z_send.at[sweep, step],
                z_recv.at[sweep, step],
                (x, y, other),
            )
            for step in range(3)
        ]
        y_copies = [
            send(partial.at[sweep, 0], carry_in.at[sweep, 0], y_send.at[sweep, 0], y_recv.at[sweep, 0], (x, y_down, z)),
            send(partial.at[sweep, 2], carry_in.at[sweep, 1], y_send.at[sweep, 1], y_recv.at[sweep, 1], (x, y_up, z)),
        ]
        for step in (0, 2, 1):
            z_copies[step].start()
        for step, copy in ((0, y_copies[0]), (2, y_copies[1])):
            z_copies[step].wait_recv()
            partial[sweep, step] = partial[sweep, step] + depth_in[sweep, step]
            copy.start()
        z_copies[1].wait_recv()
        for copy in y_copies:
            copy.wait_recv()
        for block in range(nblocks):
            for k in range(3):
                lanes = pl.ds(k * BLOCK, BLOCK)
                total = (
                    partial[sweep, 1, block, :, lanes]
                    + depth_in[sweep, 1, block, :, lanes]
                    + (carry_in[sweep, 0, block, :, lanes] + carry_in[sweep, 1, block, :, lanes])
                )
                out_ref[block, :, lanes] = respond(
                    field_ref[block, :, lanes] + coupling * total, block
                )

        @pl.when(sweep < ITERS - 1)
        def _():
            sources[sweep + 1, 1] = out_ref[...]
            for copy in x_copies(sweep + 1):
                copy.start()

        for copy in z_copies:
            copy.wait_send()
        for copy in y_copies:
            copy.wait_send()
        return carried

    lax.fori_loop(0, ITERS, sweep_step, 0)


def shards(positions, polarizability, applied_field, pair_codes, pair_counts):
    freqs = polarizability.shape[0]
    nblocks = positions.shape[1] // BLOCK
    pairs = pair_codes.shape[0]
    rows = 2 * freqs
    sizes = (lax.axis_size("gx"), lax.axis_size("gy"), nblocks, pairs)
    pos = positions.reshape(3, nblocks, BLOCK).transpose(1, 0, 2)
    pos = jnp.pad(pos, ((0, 0), (0, 5), (0, 0)))
    alpha = polarizability.reshape(freqs, 2, nblocks, BLOCK).transpose(2, 1, 0, 3)
    a1 = jnp.concatenate([alpha[:, 0], alpha[:, 0]], axis=1)
    a2 = jnp.concatenate([-alpha[:, 1], alpha[:, 1]], axis=1)
    field = applied_field.reshape(freqs, 2, 3, nblocks, BLOCK).transpose(3, 1, 0, 2, 4)
    field = field.reshape(nblocks, rows, 3 * BLOCK)
    vmem = pl.BlockSpec(memory_space=pltpu.VMEM)
    smem = pl.BlockSpec(memory_space=pltpu.SMEM)
    wide = 3 * BLOCK
    dma = pltpu.SemaphoreType.DMA
    out = pl.pallas_call(
        functools.partial(kernel, sizes),
        out_shape=jax.ShapeDtypeStruct((nblocks, rows, wide), jnp.float32),
        in_specs=[smem, smem, vmem, vmem, vmem, vmem],
        out_specs=vmem,
        scratch_shapes=[
            pltpu.VMEM((3, nblocks, 8, BLOCK), jnp.float32),
            pltpu.VMEM((6, nblocks, 8, BLOCK), jnp.float32),
            pltpu.VMEM((pairs, 2 * wide, wide), jnp.bfloat16),
            pltpu.VMEM((pairs * rows, 6 * nblocks * rows), jnp.float32),
            pltpu.VMEM((6 * nblocks * rows, pairs * rows), jnp.bfloat16),
            pltpu.VMEM((ITERS, 3, nblocks, rows, wide), jnp.float32),
            pltpu.VMEM((3, nblocks, 2 * rows, wide), jnp.bfloat16),
            pltpu.VMEM((pairs * rows, wide), jnp.float32),
            pltpu.VMEM((ITERS, 6, nblocks, rows, wide), jnp.float32),
            pltpu.VMEM((ITERS, 3, nblocks, rows, wide), jnp.float32),
            pltpu.VMEM((ITERS, 2, nblocks, rows, wide), jnp.float32),
            dma((7,)),
            dma((7,)),
            dma((ITERS, 2)),
            dma((ITERS, 2)),
            dma((ITERS, 3)),
            dma((ITERS, 3)),
            dma((ITERS, 2)),
            dma((ITERS, 2)),
        ],
        compiler_params=pltpu.CompilerParams(
            collective_id=0, has_side_effects=True, vmem_limit_bytes=40 * 1024 * 1024
        ),
    )(pair_codes, pair_counts, pos, a1, a2, field)
    out = out.reshape(nblocks, 2, freqs, 3, BLOCK).transpose(2, 1, 3, 0, 4)
    return out.reshape(freqs, 2, 3, nblocks * BLOCK)


def solution(mesh):
    in_specs = (
        P(None, ("gx", "gy", "gz")),
        P(None, None, ("gx", "gy", "gz")),
        P(None, None, None, ("gx", "gy", "gz")),
        P(("gx", "gy", "gz")),
        P(("gx", "gy", "gz")),
    )
    out_specs = P(None, None, None, ("gx", "gy", "gz"))
    return jax.shard_map(shards, mesh=mesh, in_specs=in_specs, out_specs=out_specs, check_vma=False)
```

time: 820 us -> 84.5 us (0.10)
  waiting for transfers between devices: 564 us -> 0 us
  loops' own time: 135 us -> 0 us
  Pallas kernels: 0 us -> 80.1 us
  starting transfers between devices: 35 us -> 0 us
  local copies, waits for them, and re-layouts: 32.4 us -> 3.28 us
  matrix products: 20.7 us -> 0 us
  other arithmetic: 17.2 us -> 0.02 us
  between operations: 13.5 us -> 0.77 us
    unnamed x8 -> x0, waiting for transfers between devices: 522 us -> none
    another operation x4 -> x0, loops' own time: 135 us -> none  [shards(): partial_value = lax.fori_loop(0, pair_counts[0], own_entry, partial_value)]
    pallas_call x0 -> x1, Pallas kernels: none -> 80.1 us  [shards(): pl.pallas_call(functools.partial(kernel, sizes), out_shape=jax.ShapeDtype...]
    ppermute x22 -> x0, waiting for transfers between devices: 42.3 us -> none  [the longest x8 26 us: from_behind(): return lax.ppermute(value, axis, pairs)]
    ppermute x22 -> x0, starting transfers between devices: 34.9 us -> none  [the longest x8 14.6 us: from_behind(): return lax.ppermute(value, axis, pairs)]
    dot_general x28 -> x0, matrix products: 20.7 us -> none  [tensor_field(): lax.dot_general(flat_src, matrix, (((1,), (1,)), ((), ())), precision=lax...]
    dynamic_slice x56 -> x0, local copies, waits for them, and re-layouts: 17.5 us -> none  [the longest x28 17.2 us: own_entry(): return add_pair(partial_value, pair_codes[entry], sources, z_index)]
    mul x56 -> x0, other arithmetic: 9.36 us -> none  [the longest x28 8.55 us: tensor_field(): (3.0 * screened * inv_sq * inv_dist + gaussian * (2.0 * screen * screen +...]
  transfers between devices with their start and end apart: 26 -> 0, of which waited for: 21 -> 0; matrix products, arithmetic and copies ran while one was open for 0% -> 0% of each run, Pallas kernels for 0% -> 0%
where the time goes in v1:
time: 84.5 us; the launch traced here: 84.2 us
  Pallas kernels  80.1 us (95%)
  local copies, waits for them, and re-layouts  3.28 us (4%)
    pallas_call x1, Pallas kernels, shards(): pl.pallas_call(functools.partial(kernel, sizes), out_shape=jax.ShapeDtype...  80.1 us

profile of v1, /device:TPU:0, one launch (start us, length us, event | category | flops | bytes accessed | tf_op | source)
XLA Modules:
  0.0 84.2 jit_solution(13645952711551093407)
XLA Ops:
  0.0 0.8 reshape.19
  0.8 0.0 copy-start.1
  0.9 0.8 copy-done.1
  1.7 0.1 reshape.20
  1.8 0.1 copy.15
  1.8 0.0 copy-start.2
  1.9 0.1 reshape.21.field_ref
  1.9 0.6 copy-done.2
  2.6 0.0 copy-start
  3.2 0.0 copy-done
  3.3 80.1 %shard_map.55 = f32[8,8,384]{2,1,0:T(8,128)S(1)} custom-call(s32[24]{0:T(128)S(1)} %copy-done, s32[1]{0:T(128)S(6)} %copy.17.count_ref, f32[8,8,128]{2,1,0:T(8,128)S(1)} %pad.4.pos_ref, f32[8,8,128]{2,1,0:T(8,128)S(1)} %get-tuple-element.7.a1_ref, f32[8,8,128]{2,1,0:T(8,128)S(1)} %get-tuple-element.8.a2_ref, f32[8,8,384]{2,1,0:T(8,128)S(1)} %reshape.21.field_ref), custom_call_target="tpu_custom_call" | custom-call | tf_op jit(solution)/shard_map/pallas_call | solution.py:287
  83.5 0.1 copy.12
  83.5 0.7 reshape.23
  (6 shorter events, 0.1 us)
Async XLA Ops:
  0.8 0.9 %copy-start.1 = (f32[4,2,3,1024]{3,1,2,0:T(2,128)S(1)}, f32[4,2,3,1024]{3,1,2,0:T(2,128)}, u32[]{:S(2)}) copy-start(f32[4,2,3,1024]{3,1,2,0:T(2,128)} %param.7) | copy-start | bytes 294916
  1.8 0.7 copy-start.2
  2.6 0.7 copy-start

commit v2 on v1

--- a/solution.py
+++ b/solution.py
@@ -10,7 +10,7 @@
 
 BLOCK = 128
 ITERS = 4
-UNROLL = 4
+UNROLL = 8
 
 cell_width = 4.0
 soften = 1.0
@@ -72,7 +72,7 @@
 ):
     n_x, n_y, nblocks, pairs = sizes
     square = nblocks * nblocks
-    rows = field_ref.shape[1]
+    rows = field_ref.shape[2]
     x = lax.axis_index("gx")
     y = lax.axis_index("gy")
     z = lax.axis_index("gz")
@@ -97,10 +97,9 @@
         turned = jnp.concatenate([field[rows // 2 :], field[: rows // 2]], axis=0)
         return a1_ref[block] * field + a2_ref[block] * turned
 
-    for block in range(nblocks):
-        for k in range(3):
-            lanes = pl.ds(k * BLOCK, BLOCK)
-            sources[0, 1, block, :, lanes] = respond(field_ref[block, :, lanes], block)
+    for k in range(3):
+        for block in range(nblocks):
+            sources[0, 1, k, block] = respond(field_ref[k, block], block)
     src_pos[1] = pos_ref[...]
     tgt_pos[1] = pos_ref[...]
 
@@ -116,10 +115,11 @@
 
     pl.semaphore_wait(barrier, len(partners))
 
-    def x_copies(sweep):
+    def x_copies(sweep, k):
+        own = sources.at[sweep, 1, k]
         return (
-            send(sources.at[sweep, 1], sources.at[sweep, 0], x_send.at[sweep, 0], x_recv.at[sweep, 0], (x_up, y, z)),
-            send(sources.at[sweep, 1], sources.at[sweep, 2], x_send.at[sweep, 1], x_recv.at[sweep, 1], (x_down, y, z)),
+            send(own, sources.at[sweep, 0, k], x_send.at[sweep, k, 0], x_recv.at[sweep, k, 0], (x_up, y, z)),
+            send(own, sources.at[sweep, 2, k], x_send.at[sweep, k, 1], x_recv.at[sweep, k, 1], (x_down, y, z)),
         )
 
     pos_copies = (
@@ -133,8 +133,9 @@
     )
     for copy in pos_copies:
         copy.start()
-    for copy in x_copies(0):
-        copy.start()
+    for k in range(3):
+        for copy in x_copies(0, k):
+            copy.start()
     for copy in pos_copies:
         copy.wait()
 
@@ -178,8 +179,8 @@
                 high, low = split(value)
                 for r, c in {(a, b), (b, a)}:
                     lanes = pl.ds(c * BLOCK, BLOCK)
-                    tensors[entry, pl.ds(r * BLOCK, BLOCK), lanes] = high
-                    tensors[entry, pl.ds((3 + r) * BLOCK, BLOCK), lanes] = low
+                    tensors[entry, r, pl.ds(0, BLOCK), lanes] = high
+                    tensors[entry, r, pl.ds(BLOCK, BLOCK), lanes] = low
         slot = (depth * 3 + step_y) * nblocks + tgt_block
         slot = jnp.where(entry < count_ref[0], slot, -1)
         shape = (rows, 6 * nblocks * rows)
@@ -192,76 +193,90 @@
     chosen[...] = choose[...].T.astype(jnp.bfloat16)
 
     def sweep_step(sweep, carried):
-        copies = x_copies(sweep)
-        for copy in copies:
-            copy.wait()
-        for step in range(3):
-            for block in range(nblocks):
-                high, low = split(sources[sweep, step, block])
-                halves[step, block] = jnp.concatenate([high, low], axis=0)
-
-        def pair_step(group, carried):
-            for member in range(UNROLL):
-                entry = group * UNROLL + member
-                src_block, _, _, _, step_x = decode(entry)
-                both = halves[step_x, src_block]
-                both = jnp.concatenate([both, both], axis=1)
-                result = jnp.dot(both, tensors[entry], preferred_element_type=jnp.float32)
-                contribs[pl.ds(entry * rows, rows), :] = result[:rows] + result[rows:]
-            return carried
-
-        lax.fori_loop(0, pairs // UNROLL, pair_step, 0)
-        high, low = split(contribs[...])
-        merged = jnp.dot(chosen[...], high, preferred_element_type=jnp.float32) + jnp.dot(
-            chosen[...], low, preferred_element_type=jnp.float32
-        )
-        partial[sweep] = merged.reshape(6, nblocks, rows, 3 * BLOCK)
+        for k in range(3):
+            for copy in x_copies(sweep, k):
+                copy.wait()
+            for step in range(3):
+                for block in range(nblocks):
+                    high, low = split(sources[sweep, step, k, block])
+                    halves[k, step, block] = jnp.concatenate([high, low], axis=0)
+
+            def pair_step(group, carried):
+                for member in range(UNROLL):
+                    entry = group * UNROLL + member
+                    src_block, _, _, _, step_x = decode(entry)
+                    both = halves[k, step_x, src_block]
+                    both = jnp.concatenate([both, both], axis=1)
+                    result = jnp.dot(both, tensors[entry, k], preferred_element_type=jnp.float32)
+                    result = result[:rows] + result[rows:]
+                    place = pl.ds(entry * rows, rows)
+                    contribs[place, :] = result if k == 0 else contribs[place, :] + result
+                return carried
+
+            lax.fori_loop(0, pairs // UNROLL, pair_step, 0)
 
         z_copies = [
             send(
-                partial.at[sweep, 3 + step],
-                depth_in.at[sweep, step],
-                z_send.at[sweep, step],
-                z_recv.at[sweep, step],
+                partial.at[sweep, k, pl.ds(3, 3)],
+                depth_in.at[sweep, k],
+                z_send.at[sweep, k],
+                z_recv.at[sweep, k],
                 (x, y, other),
             )
-            for step in range(3)
+            for k in range(3)
         ]
         y_copies = [
-            send(partial.at[sweep, 0], carry_in.at[sweep, 0], y_send.at[sweep, 0], y_recv.at[sweep, 0], (x, y_down, z)),
-            send(partial.at[sweep, 2], carry_in.at[sweep, 1], y_send.at[sweep, 1], y_recv.at[sweep, 1], (x, y_up, z)),
+            (
+                send(
+                    partial.at[sweep, k, 0],
+                    carry_in.at[sweep, k, 0],
+                    y_send.at[sweep, k, 0],
+                    y_recv.at[sweep, k, 0],
+                    (x, y_down, z),
+                ),
+                send(
+                    partial.at[sweep, k, 2],
+                    carry_in.at[sweep, k, 1],
+                    y_send.at[sweep, k, 1],
+                    y_recv.at[sweep, k, 1],
+                    (x, y_up, z),
+                ),
+            )
+            for k in range(3)
         ]
-        for step in (0, 2, 1):
-            z_copies[step].start()
-        for step, copy in ((0, y_copies[0]), (2, y_copies[1])):
-            z_copies[step].wait_recv()
-            partial[sweep, step] = partial[sweep, step] + depth_in[sweep, step]
-            copy.start()
-        z_copies[1].wait_recv()
-        for copy in y_copies:
-            copy.wait_recv()
-        for block in range(nblocks):
-            for k in range(3):
-                lanes = pl.ds(k * BLOCK, BLOCK)
+        for k in range(3):
+            high, low = split(contribs[:, pl.ds(k * BLOCK, BLOCK)])
+            both = jnp.concatenate([high, low], axis=1)
+            merged = jnp.dot(chosen[...], both, preferred_element_type=jnp.float32)
+            merged = merged[:, :BLOCK] + merged[:, BLOCK:]
+            partial[sweep, k] = merged.reshape(6, nblocks, rows, BLOCK)
+            z_copies[k].start()
+        for k in range(3):
+            z_copies[k].wait_recv()
+            for step, copy in zip((0, 2), y_copies[k]):
+                partial[sweep, k, step] = partial[sweep, k, step] + depth_in[sweep, k, step]
+                copy.start()
+        for k in range(3):
+            for copy in y_copies[k]:
+                copy.wait_recv()
+            for block in range(nblocks):
                 total = (
-                    partial[sweep, 1, block, :, lanes]
-                    + depth_in[sweep, 1, block, :, lanes]
-                    + (carry_in[sweep, 0, block, :, lanes] + carry_in[sweep, 1, block, :, lanes])
+                    partial[sweep, k, 1, block]
+                    + depth_in[sweep, k, 1, block]
+                    + (carry_in[sweep, k, 0, block] + carry_in[sweep, k, 1, block])
                 )
-                out_ref[block, :, lanes] = respond(
-                    field_ref[block, :, lanes] + coupling * total, block
-                )
-
-        @pl.when(sweep < ITERS - 1)
-        def _():
-            sources[sweep + 1, 1] = out_ref[...]
-            for copy in x_copies(sweep + 1):
-                copy.start()
-
-        for copy in z_copies:
-            copy.wait_send()
-        for copy in y_copies:
-            copy.wait_send()
+                out_ref[k, block] = respond(field_ref[k, block] + coupling * total, block)
+
+            @pl.when(sweep < ITERS - 1)
+            def _():
+                sources[sweep + 1, 1, k] = out_ref[k]
+                for copy in x_copies(sweep + 1, k):
+                    copy.start()
+
+        for k in range(3):
+            z_copies[k].wait_send()
+            for copy in y_copies[k]:
+                copy.wait_send()
         return carried
 
     lax.fori_loop(0, ITERS, sweep_step, 0)
@@ -278,43 +293,43 @@
     alpha = polarizability.reshape(freqs, 2, nblocks, BLOCK).transpose(2, 1, 0, 3)
     a1 = jnp.concatenate([alpha[:, 0], alpha[:, 0]], axis=1)
     a2 = jnp.concatenate([-alpha[:, 1], alpha[:, 1]], axis=1)
-    field = applied_field.reshape(freqs, 2, 3, nblocks, BLOCK).transpose(3, 1, 0, 2, 4)
-    field = field.reshape(nblocks, rows, 3 * BLOCK)
+    field = applied_field.reshape(freqs, 2, 3, nblocks, BLOCK).transpose(2, 3, 1, 0, 4)
+    field = field.reshape(3, nblocks, rows, BLOCK)
     vmem = pl.BlockSpec(memory_space=pltpu.VMEM)
     smem = pl.BlockSpec(memory_space=pltpu.SMEM)
     wide = 3 * BLOCK
     dma = pltpu.SemaphoreType.DMA
     out = pl.pallas_call(
         functools.partial(kernel, sizes),
-        out_shape=jax.ShapeDtypeStruct((nblocks, rows, wide), jnp.float32),
+        out_shape=jax.ShapeDtypeStruct((3, nblocks, rows, BLOCK), jnp.float32),
         in_specs=[smem, smem, vmem, vmem, vmem, vmem],
         out_specs=vmem,
         scratch_shapes=[
             pltpu.VMEM((3, nblocks, 8, BLOCK), jnp.float32),
             pltpu.VMEM((6, nblocks, 8, BLOCK), jnp.float32),
-            pltpu.VMEM((pairs, 2 * wide, wide), jnp.bfloat16),
+            pltpu.VMEM((pairs, 3, 2 * BLOCK, wide), jnp.bfloat16),
             pltpu.VMEM((pairs * rows, 6 * nblocks * rows), jnp.float32),
             pltpu.VMEM((6 * nblocks * rows, pairs * rows), jnp.bfloat16),
-            pltpu.VMEM((ITERS, 3, nblocks, rows, wide), jnp.float32),
-            pltpu.VMEM((3, nblocks, 2 * rows, wide), jnp.bfloat16),
+            pltpu.VMEM((ITERS, 3, 3, nblocks, rows, BLOCK), jnp.float32),
+            pltpu.VMEM((3, 3, nblocks, 2 * rows, BLOCK), jnp.bfloat16),
             pltpu.VMEM((pairs * rows, wide), jnp.float32),
-            pltpu.VMEM((ITERS, 6, nblocks, rows, wide), jnp.float32),
-            pltpu.VMEM((ITERS, 3, nblocks, rows, wide), jnp.float32),
-            pltpu.VMEM((ITERS, 2, nblocks, rows, wide), jnp.float32),
+            pltpu.VMEM((ITERS, 3, 6, nblocks, rows, BLOCK), jnp.float32),
+            pltpu.VMEM((ITERS, 3, 3, nblocks, rows, BLOCK), jnp.float32),
+            pltpu.VMEM((ITERS, 3, 2, nblocks, rows, BLOCK), jnp.float32),
             dma((7,)),
             dma((7,)),
-            dma((ITERS, 2)),
-            dma((ITERS, 2)),
+            dma((ITERS, 3, 2)),
+            dma((ITERS, 3, 2)),
             dma((ITERS, 3)),
             dma((ITERS, 3)),
-            dma((ITERS, 2)),
-            dma((ITERS, 2)),
+            dma((ITERS, 3, 2)),
+            dma((ITERS, 3, 2)),
         ],
         compiler_params=pltpu.CompilerParams(
             collective_id=0, has_side_effects=True, vmem_limit_bytes=40 * 1024 * 1024
         ),
     )(pair_codes, pair_counts, pos, a1, a2, field)
-    out = out.reshape(nblocks, 2, freqs, 3, BLOCK).transpose(2, 1, 3, 0, 4)
+    out = out.reshape(3, nblocks, 2, freqs, BLOCK).transpose(3, 2, 0, 1, 4)
     return out.reshape(freqs, 2, 3, nblocks * BLOCK)
 
 

time: 84.5 us -> 73.9 us (0.87)
  Pallas kernels: 80.1 us -> 69.8 us
    pallas_call x1, Pallas kernels: 80.1 us -> 69.8 us  [shards(): pl.pallas_call(functools.partial(kernel, sizes), out_shape=jax.ShapeDtype...]
where the time goes in v2:
time: 73.9 us; the launch traced here: 73.6 us
  Pallas kernels  69.8 us (94%)
  local copies, waits for them, and re-layouts  3.11 us (4%)
  between operations  0.74 us (1%)
    pallas_call x1, Pallas kernels, shards(): pl.pallas_call(functools.partial(kernel, sizes), out_shape=jax.ShapeDtype...  69.8 us
    unnamed x6, local copies, waits for them, and re-layouts  1.5 us

profile of v2, /device:TPU:0, one launch (start us, length us, event | category | flops | bytes accessed | tf_op | source)
XLA Modules:
  0.0 73.6 jit_solution(13970690690049198885)
XLA Ops:
  0.0 0.0 copy-start.2
  0.7 0.7 pad.4.pos_ref
  1.4 0.0 copy-done.2
  1.5 0.0 copy-start.1
  1.5 0.8 %copy-done.1 = f32[4,2,3,1024]{3,1,2,0:T(2,128)S(1)} copy-done((f32[4,2,3,1024]{3,1,2,0:T(2,128)S(1)}, f32[4,2,3,1024]{3,1,2,0:T(2,128)}, u32[]{:S(2)}) %copy-start.1) | copy-done | bytes 98328
  2.4 0.1 reshape.20
  2.5 0.0 copy-start
  2.5 0.6 copy-done
  3.1 69.8 %shard_map.55 = f32[3,8,8,128]{3,2,1,0:T(8,128)S(1)} custom-call(s32[24]{0:T(128)S(1)} %copy-done, s32[1]{0:T(128)S(6)} %copy.13.count_ref, f32[8,8,128]{2,1,0:T(8,128)S(1)} %pad.4.pos_ref, f32[8,8,128]{2,1,0:T(8,128)S(1)} %get-tuple-element.7.a1_ref, f32[8,8,128]{2,1,0:T(8,128)S(1)} %get-tuple-element.8.a2_ref, f32[3,8,8,128]{3,2,1,0:T(8,128)S(1)} %bitcast.24), custom_call_target="tpu_custom_call" | custom-call | tf_op jit(solution)/shard_map/pallas_call | solution.py:302
  72.9 0.7 reshape.23
  (7 shorter events, 0.1 us)
Async XLA Ops:
  0.0 1.4 %copy-start.2 = (f32[4,2,1024]{2,1,0:T(2,128)S(1)}, f32[4,2,1024]{2,1,0:T(2,128)}, u32[]{:S(2)}) copy-start(f32[4,2,1024]{2,1,0:T(2,128)} %param.6) | copy-start | bytes 98308
  1.5 0.9 %copy-start.1 = (f32[4,2,3,1024]{3,1,2,0:T(2,128)S(1)}, f32[4,2,3,1024]{3,1,2,0:T(2,128)}, u32[]{:S(2)}) copy-start(f32[4,2,3,1024]{3,1,2,0:T(2,128)} %param.7) | copy-start | bytes 294916
  2.5 0.7 copy-start

commit v3 on v2

--- a/solution.py
+++ b/solution.py
@@ -170,17 +170,14 @@
         scale = jnp.exp(-screen * screen * dist_sq) * inv_sq
         b_term = scale * series
         c_term = scale * (3.0 * inv_sq * series + 2.0 * screen * screen / math.sqrt(math.pi))
-        for a in range(3):
-            scaled = c_term * disp[a]
-            for b in range(a, 3):
-                value = scaled * disp[b]
-                if a == b:
-                    value = value - b_term
+        for t in range(3):
+            scaled = c_term * disp[t]
+            pieces = (scaled * disp[t] - b_term, scaled * disp[(t + 1) % 3])
+            for part, value in enumerate(pieces):
                 high, low = split(value)
-                for r, c in {(a, b), (b, a)}:
-                    lanes = pl.ds(c * BLOCK, BLOCK)
-                    tensors[entry, r, pl.ds(0, BLOCK), lanes] = high
-                    tensors[entry, r, pl.ds(BLOCK, BLOCK), lanes] = low
+                lanes = pl.ds(part * BLOCK, BLOCK)
+                tensors[entry, t, pl.ds(0, BLOCK), lanes] = high
+                tensors[entry, t, pl.ds(BLOCK, BLOCK), lanes] = low
         slot = (depth * 3 + step_y) * nblocks + tgt_block
         slot = jnp.where(entry < count_ref[0], slot, -1)
         shape = (rows, 6 * nblocks * rows)
@@ -193,27 +190,60 @@
     chosen[...] = choose[...].T.astype(jnp.bfloat16)
 
     def sweep_step(sweep, carried):
-        for k in range(3):
+        def arrive(k):
             for copy in x_copies(sweep, k):
                 copy.wait()
             for step in range(3):
                 for block in range(nblocks):
                     high, low = split(sources[sweep, step, k, block])
-                    halves[k, step, block] = jnp.concatenate([high, low], axis=0)
-
-            def pair_step(group, carried):
-                for member in range(UNROLL):
-                    entry = group * UNROLL + member
-                    src_block, _, _, _, step_x = decode(entry)
-                    both = halves[k, step_x, src_block]
-                    both = jnp.concatenate([both, both], axis=1)
-                    result = jnp.dot(both, tensors[entry, k], preferred_element_type=jnp.float32)
-                    result = result[:rows] + result[rows:]
-                    place = pl.ds(entry * rows, rows)
-                    contribs[place, :] = result if k == 0 else contribs[place, :] + result
-                return carried
-
-            lax.fori_loop(0, pairs // UNROLL, pair_step, 0)
+                    both = jnp.concatenate([high, low], axis=0)
+                    halves[step, block, pl.ds(k * 2 * rows, 2 * rows)] = both
+
+        def tile_dot(entry, t, step_x, src_block):
+            if t < 2:
+                both = halves[step_x, src_block, pl.ds(t * 2 * rows, 4 * rows)]
+            else:
+                both = jnp.concatenate(
+                    [
+                        halves[step_x, src_block, pl.ds(4 * rows, 2 * rows)],
+                        halves[step_x, src_block, pl.ds(0, 2 * rows)],
+                    ],
+                    axis=0,
+                )
+            both = jnp.concatenate([both, both], axis=1)
+            result = jnp.dot(both, tensors[entry, t], preferred_element_type=jnp.float32)
+            first = result[:rows] + result[rows : 2 * rows]
+            second = result[2 * rows : 3 * rows, BLOCK:] + result[3 * rows :, BLOCK:]
+            return first[:, :BLOCK] + second, first[:, BLOCK:]
+
+        def early_step(group, carried):
+            for member in range(UNROLL):
+                entry = group * UNROLL + member
+                src_block, _, _, _, step_x = decode(entry)
+                to_x, to_y = tile_dot(entry, 0, step_x, src_block)
+                place = pl.ds(entry * rows, rows)
+                contribs[place, pl.ds(0, BLOCK)] = to_x
+                contribs[place, pl.ds(BLOCK, BLOCK)] = to_y
+            return carried
+
+        def late_step(group, carried):
+            for member in range(UNROLL):
+                entry = group * UNROLL + member
+                src_block, _, _, _, step_x = decode(entry)
+                to_y, from_y = tile_dot(entry, 1, step_x, src_block)
+                to_z, to_x = tile_dot(entry, 2, step_x, src_block)
+                place = pl.ds(entry * rows, rows)
+                lanes = [pl.ds(k * BLOCK, BLOCK) for k in range(3)]
+                contribs[place, lanes[0]] = contribs[place, lanes[0]] + to_x
+                contribs[place, lanes[1]] = contribs[place, lanes[1]] + to_y
+                contribs[place, lanes[2]] = from_y + to_z
+            return carried
+
+        arrive(0)
+        arrive(1)
+        lax.fori_loop(0, pairs // UNROLL, early_step, 0)
+        arrive(2)
+        lax.fori_loop(0, pairs // UNROLL, late_step, 0)
 
         z_copies = [
             send(
@@ -307,11 +337,11 @@
         scratch_shapes=[
             pltpu.VMEM((3, nblocks, 8, BLOCK), jnp.float32),
             pltpu.VMEM((6, nblocks, 8, BLOCK), jnp.float32),
-            pltpu.VMEM((pairs, 3, 2 * BLOCK, wide), jnp.bfloat16),
+            pltpu.VMEM((pairs, 3, 2 * BLOCK, 2 * BLOCK), jnp.bfloat16),
             pltpu.VMEM((pairs * rows, 6 * nblocks * rows), jnp.float32),
             pltpu.VMEM((6 * nblocks * rows, pairs * rows), jnp.bfloat16),
             pltpu.VMEM((ITERS, 3, 3, nblocks, rows, BLOCK), jnp.float32),
-            pltpu.VMEM((3, 3, nblocks, 2 * rows, BLOCK), jnp.bfloat16),
+            pltpu.VMEM((3, nblocks, 6 * rows, BLOCK), jnp.bfloat16),
             pltpu.VMEM((pairs * rows, wide), jnp.float32),
             pltpu.VMEM((ITERS, 3, 6, nblocks, rows, BLOCK), jnp.float32),
             pltpu.VMEM((ITERS, 3, 3, nblocks, rows, BLOCK), jnp.float32),

time: 73.9 us -> 74.5 us (level)
  no operation moved by 1% of the time
where the time goes in v3:
time: 74.5 us; the launch traced here: 74.3 us
  Pallas kernels  70.4 us (94%)
  local copies, waits for them, and re-layouts  3.11 us (4%)
    pallas_call x1, Pallas kernels, shards(): pl.pallas_call(functools.partial(kernel, sizes), out_shape=jax.ShapeDtype...  70.4 us
    unnamed x6, local copies, waits for them, and re-layouts  1.5 us

profile of v3, /device:TPU:0, one launch (start us, length us, event | category | flops | bytes accessed | tf_op | source)
XLA Modules:
  0.0 74.3 jit_solution(2350449813967614983)
XLA Ops:
  0.0 0.0 copy-start.2
  0.7 0.7 pad.4.pos_ref
  1.4 0.0 copy-done.2
  1.5 0.0 copy-start.1
  1.5 0.8 %copy-done.1 = f32[4,2,3,1024]{3,1,2,0:T(2,128)S(1)} copy-done((f32[4,2,3,1024]{3,1,2,0:T(2,128)S(1)}, f32[4,2,3,1024]{3,1,2,0:T(2,128)}, u32[]{:S(2)}) %copy-start.1) | copy-done | bytes 98328
  2.4 0.1 reshape.20
  2.5 0.0 copy-start
  2.5 0.6 copy-done
  3.1 70.4 %shard_map.55 = f32[3,8,8,128]{3,2,1,0:T(8,128)S(1)} custom-call(s32[24]{0:T(128)S(1)} %copy-done, s32[1]{0:T(128)S(6)} %copy.13.count_ref, f32[8,8,128]{2,1,0:T(8,128)S(1)} %pad.4.pos_ref, f32[8,8,128]{2,1,0:T(8,128)S(1)} %get-tuple-element.7.a1_ref, f32[8,8,128]{2,1,0:T(8,128)S(1)} %get-tuple-element.8.a2_ref, f32[3,8,8,128]{3,2,1,0:T(8,128)S(1)} %bitcast.24), custom_call_target="tpu_custom_call" | custom-call | tf_op jit(solution)/shard_map/pallas_call | solution.py:332
  73.6 0.7 reshape.23
  (7 shorter events, 0.1 us)
Async XLA Ops:
  0.0 1.4 %copy-start.2 = (f32[4,2,1024]{2,1,0:T(2,128)S(1)}, f32[4,2,1024]{2,1,0:T(2,128)}, u32[]{:S(2)}) copy-start(f32[4,2,1024]{2,1,0:T(2,128)} %param.6) | copy-start | bytes 98308
  1.5 0.9 %copy-start.1 = (f32[4,2,3,1024]{3,1,2,0:T(2,128)S(1)}, f32[4,2,3,1024]{3,1,2,0:T(2,128)}, u32[]{:S(2)}) copy-start(f32[4,2,3,1024]{3,1,2,0:T(2,128)} %param.7) | copy-start | bytes 294916
  2.5 0.7 copy-start

commit v4 on v3

--- a/solution.py
+++ b/solution.py
@@ -11,6 +11,7 @@
 BLOCK = 128
 ITERS = 4
 UNROLL = 8
+STRIP = 64
 
 cell_width = 4.0
 soften = 1.0
@@ -45,11 +46,13 @@
     sizes,
     codes_ref,
     count_ref,
-    pos_ref,
+    raw_pos,
+    raw_alpha,
+    raw_field,
+    out_ref,
     a1_ref,
     a2_ref,
     field_ref,
-    out_ref,
     src_pos,
     tgt_pos,
     tensors,
@@ -58,6 +61,7 @@
     sources,
     halves,
     contribs,
+    latest,
     partial,
     depth_in,
     carry_in,
@@ -97,11 +101,21 @@
         turned = jnp.concatenate([field[rows // 2 :], field[: rows // 2]], axis=0)
         return a1_ref[block] * field + a2_ref[block] * turned
 
+    src_pos[1] = jnp.zeros_like(src_pos[1])
+    for block in range(nblocks):
+        span = pl.ds(block * BLOCK, BLOCK)
+        src_pos[1, block, pl.ds(0, 3), :] = raw_pos[:, span]
+        real, imag = raw_alpha[:, 0, span], raw_alpha[:, 1, span]
+        a1_ref[block] = jnp.concatenate([real, real], axis=0)
+        a2_ref[block] = jnp.concatenate([-imag, imag], axis=0)
+        for k in range(3):
+            field_ref[k, block] = jnp.concatenate(
+                [raw_field[:, k, 0, span], raw_field[:, k, 1, span]], axis=0
+            )
+    tgt_pos[1] = src_pos[1]
     for k in range(3):
         for block in range(nblocks):
             sources[0, 1, k, block] = respond(field_ref[k, block], block)
-    src_pos[1] = pos_ref[...]
-    tgt_pos[1] = pos_ref[...]
 
     def send(src, dst, send_sem, recv_sem, device):
         return pltpu.make_async_remote_copy(
@@ -123,13 +137,13 @@
         )
 
     pos_copies = (
-        send(pos_ref, src_pos.at[0], pos_send.at[0], pos_recv.at[0], (x_up, y, z)),
-        send(pos_ref, src_pos.at[2], pos_send.at[1], pos_recv.at[1], (x_down, y, z)),
-        send(pos_ref, tgt_pos.at[0], pos_send.at[2], pos_recv.at[2], (x, y_up, z)),
-        send(pos_ref, tgt_pos.at[2], pos_send.at[3], pos_recv.at[3], (x, y_down, z)),
-        send(pos_ref, tgt_pos.at[3], pos_send.at[4], pos_recv.at[4], (x, y_up, other)),
-        send(pos_ref, tgt_pos.at[5], pos_send.at[5], pos_recv.at[5], (x, y_down, other)),
-        send(pos_ref, tgt_pos.at[4], pos_send.at[6], pos_recv.at[6], (x, y, other)),
+        send(src_pos.at[1], src_pos.at[0], pos_send.at[0], pos_recv.at[0], (x_up, y, z)),
+        send(src_pos.at[1], src_pos.at[2], pos_send.at[1], pos_recv.at[1], (x_down, y, z)),
+        send(src_pos.at[1], tgt_pos.at[0], pos_send.at[2], pos_recv.at[2], (x, y_up, z)),
+        send(src_pos.at[1], tgt_pos.at[2], pos_send.at[3], pos_recv.at[3], (x, y_down, z)),
+        send(src_pos.at[1], tgt_pos.at[3], pos_send.at[4], pos_recv.at[4], (x, y_up, other)),
+        send(src_pos.at[1], tgt_pos.at[5], pos_send.at[5], pos_recv.at[5], (x, y_down, other)),
+        send(src_pos.at[1], tgt_pos.at[4], pos_send.at[6], pos_recv.at[6], (x, y, other)),
     )
     for copy in pos_copies:
         copy.start()
@@ -155,29 +169,31 @@
         tgt = tgt_pos[depth * 3 + step_y, tgt_block]
         shift_x = (step_x - 1).astype(jnp.float32) * -cell_width
         shift_y = (step_y - 1).astype(jnp.float32) * cell_width
-        disp = [
-            tgt[0:1] - src[:, 0:1] + shift_x,
-            tgt[1:2] - src[:, 1:2] + shift_y,
-            tgt[2:3] - src[:, 2:3],
-        ]
-        dist_sq = disp[0] * disp[0] + disp[1] * disp[1] + disp[2] * disp[2] + soften * soften
-        inv = lax.rsqrt(dist_sq)
-        inv_sq = inv * inv
-        offset = inv - CENTER
-        series = jnp.full_like(offset, SERIES[-1])
-        for term in SERIES[-2::-1]:
-            series = series * offset + term
-        scale = jnp.exp(-screen * screen * dist_sq) * inv_sq
-        b_term = scale * series
-        c_term = scale * (3.0 * inv_sq * series + 2.0 * screen * screen / math.sqrt(math.pi))
-        for t in range(3):
-            scaled = c_term * disp[t]
-            pieces = (scaled * disp[t] - b_term, scaled * disp[(t + 1) % 3])
-            for part, value in enumerate(pieces):
-                high, low = split(value)
-                lanes = pl.ds(part * BLOCK, BLOCK)
-                tensors[entry, t, pl.ds(0, BLOCK), lanes] = high
-                tensors[entry, t, pl.ds(BLOCK, BLOCK), lanes] = low
+        for at in range(0, BLOCK, STRIP):
+            strip = slice(at, at + STRIP)
+            disp = [
+                tgt[0:1] - src[strip, 0:1] + shift_x,
+                tgt[1:2] - src[strip, 1:2] + shift_y,
+                tgt[2:3] - src[strip, 2:3],
+            ]
+            dist_sq = disp[0] * disp[0] + disp[1] * disp[1] + disp[2] * disp[2] + soften * soften
+            inv = lax.rsqrt(dist_sq)
+            inv_sq = inv * inv
+            offset = inv - CENTER
+            series = jnp.full_like(offset, SERIES[-1])
+            for term in SERIES[-2::-1]:
+                series = series * offset + term
+            scale = jnp.exp(-screen * screen * dist_sq) * inv_sq
+            b_term = scale * series
+            c_term = scale * (3.0 * inv_sq * series + 2.0 * screen * screen / math.sqrt(math.pi))
+            for t in range(3):
+                scaled = c_term * disp[t]
+                pieces = (scaled * disp[t] - b_term, scaled * disp[(t + 1) % 3])
+                for part, value in enumerate(pieces):
+                    high, low = split(value)
+                    lanes = pl.ds(part * BLOCK, BLOCK)
+                    tensors[entry, t, pl.ds(at, STRIP), lanes] = high
+                    tensors[entry, t, pl.ds(BLOCK + at, STRIP), lanes] = low
         slot = (depth * 3 + step_y) * nblocks + tgt_block
         slot = jnp.where(entry < count_ref[0], slot, -1)
         shape = (rows, 6 * nblocks * rows)
@@ -186,7 +202,10 @@
         choose[pl.ds(entry * rows, rows), :] = jnp.where(column == slot * rows + row, 1.0, 0.0)
         return carried
 
-    lax.fori_loop(0, pairs, build, 0)
+    def build_two(group, carried):
+        return build(group * 2 + 1, build(group * 2, carried))
+
+    lax.fori_loop(0, pairs // 2, build_two, 0)
     chosen[...] = choose[...].T.astype(jnp.bfloat16)
 
     def sweep_step(sweep, carried):
@@ -295,11 +314,12 @@
                     + depth_in[sweep, k, 1, block]
                     + (carry_in[sweep, k, 0, block] + carry_in[sweep, k, 1, block])
                 )
-                out_ref[k, block] = respond(field_ref[k, block] + coupling * total, block)
+                dipole = respond(field_ref[k, block] + coupling * total, block)
+                latest[k, block] = dipole
 
             @pl.when(sweep < ITERS - 1)
             def _():
-                sources[sweep + 1, 1, k] = out_ref[k]
+                sources[sweep + 1, 1, k] = latest[k]
                 for copy in x_copies(sweep + 1, k):
                     copy.start()
 
@@ -310,6 +330,11 @@
         return carried
 
     lax.fori_loop(0, ITERS, sweep_step, 0)
+    for k in range(3):
+        for block in range(nblocks):
+            span = pl.ds(block * BLOCK, BLOCK)
+            out_ref[:, k, 0, span] = latest[k, block, : rows // 2]
+            out_ref[:, k, 1, span] = latest[k, block, rows // 2 :]
 
 
 def shards(positions, polarizability, applied_field, pair_codes, pair_counts):
@@ -318,23 +343,20 @@
     pairs = pair_codes.shape[0]
     rows = 2 * freqs
     sizes = (lax.axis_size("gx"), lax.axis_size("gy"), nblocks, pairs)
-    pos = positions.reshape(3, nblocks, BLOCK).transpose(1, 0, 2)
-    pos = jnp.pad(pos, ((0, 0), (0, 5), (0, 0)))
-    alpha = polarizability.reshape(freqs, 2, nblocks, BLOCK).transpose(2, 1, 0, 3)
-    a1 = jnp.concatenate([alpha[:, 0], alpha[:, 0]], axis=1)
-    a2 = jnp.concatenate([-alpha[:, 1], alpha[:, 1]], axis=1)
-    field = applied_field.reshape(freqs, 2, 3, nblocks, BLOCK).transpose(2, 3, 1, 0, 4)
-    field = field.reshape(3, nblocks, rows, BLOCK)
+    field = jnp.swapaxes(applied_field, 1, 2)
     vmem = pl.BlockSpec(memory_space=pltpu.VMEM)
     smem = pl.BlockSpec(memory_space=pltpu.SMEM)
     wide = 3 * BLOCK
     dma = pltpu.SemaphoreType.DMA
     out = pl.pallas_call(
         functools.partial(kernel, sizes),
-        out_shape=jax.ShapeDtypeStruct((3, nblocks, rows, BLOCK), jnp.float32),
-        in_specs=[smem, smem, vmem, vmem, vmem, vmem],
+        out_shape=jax.ShapeDtypeStruct(field.shape, jnp.float32),
+        in_specs=[smem, smem, vmem, vmem, vmem],
         out_specs=vmem,
         scratch_shapes=[
+            pltpu.VMEM((nblocks, rows, BLOCK), jnp.float32),
+            pltpu.VMEM((nblocks, rows, BLOCK), jnp.float32),
+            pltpu.VMEM((3, nblocks, rows, BLOCK), jnp.float32),
             pltpu.VMEM((3, nblocks, 8, BLOCK), jnp.float32),
             pltpu.VMEM((6, nblocks, 8, BLOCK), jnp.float32),
             pltpu.VMEM((pairs, 3, 2 * BLOCK, 2 * BLOCK), jnp.bfloat16),
@@ -343,6 +365,7 @@
             pltpu.VMEM((ITERS, 3, 3, nblocks, rows, BLOCK), jnp.float32),
             pltpu.VMEM((3, nblocks, 6 * rows, BLOCK), jnp.bfloat16),
             pltpu.VMEM((pairs * rows, wide), jnp.float32),
+            pltpu.VMEM((3, nblocks, rows, BLOCK), jnp.float32),
             pltpu.VMEM((ITERS, 3, 6, nblocks, rows, BLOCK), jnp.float32),
             pltpu.VMEM((ITERS, 3, 3, nblocks, rows, BLOCK), jnp.float32),
             pltpu.VMEM((ITERS, 3, 2, nblocks, rows, BLOCK), jnp.float32),
@@ -358,9 +381,8 @@
         compiler_params=pltpu.CompilerParams(
             collective_id=0, has_side_effects=True, vmem_limit_bytes=40 * 1024 * 1024
         ),
-    )(pair_codes, pair_counts, pos, a1, a2, field)
-    out = out.reshape(3, nblocks, 2, freqs, BLOCK).transpose(3, 2, 0, 1, 4)
-    return out.reshape(freqs, 2, 3, nblocks * BLOCK)
+    )(pair_codes, pair_counts, positions, polarizability, field)
+    return jnp.swapaxes(out, 1, 2)
 
 
 def solution(mesh):

time: 74.5 us -> 73.3 us (0.984)
  Pallas kernels: 70.4 us -> 68.7 us
    unnamed x6 -> x9, local copies, waits for them, and re-layouts: 1.5 us -> 3.66 us
    pallas_call x1, Pallas kernels: 70.4 us -> 68.7 us  [shards(): pl.pallas_call(functools.partial(kernel, sizes), out_shape=jax.ShapeDtype...]
    reshape x5 -> x0, local copies, waits for them, and re-layouts: 0.85 us -> none  [the longest x1 0.69 us: shards(): return out.reshape(freqs, 2, 3, nblocks * BLOCK)]
where the time goes in v4:
time: 73.3 us; the launch traced here: 73 us
  Pallas kernels  68.7 us (94%)
  local copies, waits for them, and re-layouts  3.66 us (5%)
    pallas_call x1, Pallas kernels, shards(): pl.pallas_call(functools.partial(kernel, sizes), out_shape=jax.ShapeDtype...  68.7 us
    unnamed x9, local copies, waits for them, and re-layouts  3.66 us

profile of v4, /device:TPU:0, one launch (start us, length us, event | category | flops | bytes accessed | tf_op | source)
XLA Modules:
  0.0 73.0 jit_solution(17244287878521209191)
XLA Ops:
  0.7 0.0 copy-start.3
  0.7 0.6 copy-done.3
  1.3 0.0 copy-start
  1.3 0.9 %copy-done = f32[4,2,3,1024]{3,1,2,0:T(2,128)S(1)} copy-done((f32[4,2,3,1024]{3,1,2,0:T(2,128)S(1)}, f32[4,2,3,1024]{3,1,2,0:T(2,128)}, u32[]{:S(2)}) %copy-start) | copy-done | bytes 98328
  2.2 0.0 copy-start.1
  2.2 0.8 %copy-done.1 = f32[4,2,1024]{2,1,0:T(2,128)S(1)} copy-done((f32[4,2,1024]{2,1,0:T(2,128)S(1)}, f32[4,2,1024]{2,1,0:T(2,128)}, u32[]{:S(2)}) %copy-start.1) | copy-done | bytes 32792
  3.0 0.0 copy-start.2
  3.0 0.7 copy-done.2
  3.7 68.7 %shard_map.55 = f32[4,3,2,1024]{3,2,1,0:T(2,128)S(1)} custom-call(s32[24]{0:T(128)S(1)} %copy-done.3, s32[1]{0:T(128)S(6)} %copy.7.count_ref, f32[3,1024]{1,0:T(4,128)S(1)} %copy-done.2, f32[4,2,1024]{2,1,0:T(2,128)S(1)} %copy-done.1, f32[4,3,2,1024]{3,2,1,0:T(2,128)S(1)} %bitcast.3), custom_call_target="tpu_custom_call" | custom-call | tf_op jit(solution)/shard_map/pallas_call | solution.py:351
  72.4 0.6 copy.8
Async XLA Ops:
  0.7 0.7 copy-start.3
  1.3 0.9 %copy-start = (f32[4,2,3,1024]{3,1,2,0:T(2,128)S(1)}, f32[4,2,3,1024]{3,1,2,0:T(2,128)}, u32[]{:S(2)}) copy-start(f32[4,2,3,1024]{3,1,2,0:T(2,128)} %param.7) | copy-start | bytes 294916
  2.2 0.8 %copy-start.1 = (f32[4,2,1024]{2,1,0:T(2,128)S(1)}, f32[4,2,1024]{2,1,0:T(2,128)}, u32[]{:S(2)}) copy-start(f32[4,2,1024]{2,1,0:T(2,128)} %raw_alpha.1) | copy-start | bytes 98308
  3.0 0.7 copy-start.2

commit v5 on v4

--- a/solution.py
+++ b/solution.py
@@ -46,10 +46,14 @@
     sizes,
     codes_ref,
     count_ref,
+    pos_hbm,
+    alpha_hbm,
+    field_hbm,
+    out_ref,
     raw_pos,
     raw_alpha,
     raw_field,
-    out_ref,
+    fetched,
     a1_ref,
     a2_ref,
     field_ref,
@@ -84,6 +88,13 @@
     y_up, y_down = lax.rem(y + 1, n_y), lax.rem(y + n_y - 1, n_y)
     other = 1 - z
 
+    fetches = (
+        pltpu.make_async_copy(pos_hbm, raw_pos, fetched.at[0]),
+        pltpu.make_async_copy(alpha_hbm, raw_alpha, fetched.at[1]),
+        pltpu.make_async_copy(field_hbm, raw_field, fetched.at[2]),
+    )
+    for fetch in fetches:
+        fetch.start()
     barrier = pltpu.get_barrier_semaphore()
     partners = (
         (x_up, y, z),
@@ -102,6 +113,8 @@
         return a1_ref[block] * field + a2_ref[block] * turned
 
     src_pos[1] = jnp.zeros_like(src_pos[1])
+    for fetch in fetches:
+        fetch.wait()
     for block in range(nblocks):
         span = pl.ds(block * BLOCK, BLOCK)
         src_pos[1, block, pl.ds(0, 3), :] = raw_pos[:, span]
@@ -345,15 +358,20 @@
     sizes = (lax.axis_size("gx"), lax.axis_size("gy"), nblocks, pairs)
     field = jnp.swapaxes(applied_field, 1, 2)
     vmem = pl.BlockSpec(memory_space=pltpu.VMEM)
+    hbm = pl.BlockSpec(memory_space=pltpu.HBM)
     smem = pl.BlockSpec(memory_space=pltpu.SMEM)
     wide = 3 * BLOCK
     dma = pltpu.SemaphoreType.DMA
     out = pl.pallas_call(
         functools.partial(kernel, sizes),
         out_shape=jax.ShapeDtypeStruct(field.shape, jnp.float32),
-        in_specs=[smem, smem, vmem, vmem, vmem],
+        in_specs=[smem, smem, hbm, hbm, hbm],
         out_specs=vmem,
         scratch_shapes=[
+            pltpu.VMEM(positions.shape, jnp.float32),
+            pltpu.VMEM(polarizability.shape, jnp.float32),
+            pltpu.VMEM(field.shape, jnp.float32),
+            dma((3,)),
             pltpu.VMEM((nblocks, rows, BLOCK), jnp.float32),
             pltpu.VMEM((nblocks, rows, BLOCK), jnp.float32),
             pltpu.VMEM((3, nblocks, rows, BLOCK), jnp.float32),
@@ -379,7 +397,7 @@
             dma((ITERS, 3, 2)),
         ],
         compiler_params=pltpu.CompilerParams(
-            collective_id=0, has_side_effects=True, vmem_limit_bytes=40 * 1024 * 1024
+            collective_id=0, has_side_effects=True, vmem_limit_bytes=64 * 1024 * 1024
         ),
     )(pair_codes, pair_counts, positions, polarizability, field)
     return jnp.swapaxes(out, 1, 2)

time: 73.3 us -> 71.9 us (0.981)
  local copies, waits for them, and re-layouts: 3.66 us -> 1.54 us
  Pallas kernels: 68.7 us -> 69.5 us
    unnamed x9 -> x1, local copies, waits for them, and re-layouts: 3.66 us -> 1.54 us
    pallas_call x1, Pallas kernels: 68.7 us -> 69.5 us  [shards(): pl.pallas_call(functools.partial(kernel, sizes), out_shape=jax.ShapeDtype...]
where the time goes in v5:
time: 71.9 us; the launch traced here: 71.7 us
  Pallas kernels  69.5 us (97%)
  local copies, waits for them, and re-layouts  1.54 us (2%)
    pallas_call x1, Pallas kernels, shards(): pl.pallas_call(functools.partial(kernel, sizes), out_shape=jax.ShapeDtype...  69.5 us
    unnamed x1, local copies, waits for them, and re-layouts  1.54 us

profile of v5, /device:TPU:0, one launch (start us, length us, event | category | flops | bytes accessed | tf_op | source)
XLA Modules:
  0.0 71.7 jit_solution(17195047443611467897)
XLA Ops:
  0.7 69.5 %shard_map.55 = f32[4,3,2,1024]{3,2,1,0:T(2,128)} custom-call(s32[24]{0:T(128)} %codes_ref.1, s32[1]{0:T(128)S(6)} %copy.7.count_ref, f32[3,1024]{1,0:T(4,128)} %pos_hbm.1, f32[4,2,1024]{2,1,0:T(2,128)} %alpha_hbm.1, f32[4,3,2,1024]{3,2,1,0:T(2,128)} %bitcast.3), custom_call_target="tpu_custom_call" | custom-call | tf_op jit(solution)/shard_map/pallas_call | solution.py:365
  70.2 1.5 %copy.8 = f32[4,2,3,1024]{3,1,2,0:T(2,128)} copy(f32[4,2,3,1024]{3,1,2,0:T(2,128)} %bitcast.2) | data formatting | bytes 196608
